TPU v7x, 32 devices: a whole 2x2x4 slice. The times are simulated.
32 devices in a mesh: row: 4 (over y, x), col: 8 (over z, core).
Axes of the slice: x: 2, y: 2, z: 4, core: 2. Of those that a mesh axis runs over, the one named last changes fastest.
Arguments:
- member_outputs: float32 [3, 8192, 512], P(None, ('row', 'col')), may hold values from -6 to 6
- pivot_inverse_matrices: bfloat16 [2, 8192, 8192], P(None, 'col', 'row'), may hold values from -1 to 1.25, as said below
- former_subdiagonal_tiles: bfloat16 [2, 8192, 8192], P(None, 'row', 'col'), may hold values from -0.09375 to 0.09375
- latter_subdiagonal_tiles: bfloat16 [1, 8192, 8192], P(None, 'row', 'col'), may hold values from -0.09375 to 0.09375
Outputs:
- whitened: bfloat16 [2, 8192, 512], P(None, 'col')
- trailing: float32 [1, 8192, 512], P(None, ('row', 'col'))
- projections: float32 [256, 512], replicated
Inputs may be any that keep to these rules, and one draw needn't show every extreme that they name: `pivot_inverse_matrices`: each block is lower triangular with a positive diagonal: the inverse of a diagonal block of the error covariance's Cholesky factor.
All inputs are finite; a program needn't handle non-finite values.
Results may differ from a plain program's by a relative error of at most 0.0057.
Values may be sent and summed in bfloat16 or wider, within the bound.
A program may use at most 64 MiB of HBM per device.

v0:
```python
import jax
import jax.numpy as jnp
from jax import lax
from jax.sharding import PartitionSpec as P


def standardize_prior_deviations(partition_height, reciprocal_matrix):
    partial_value = jnp.dot(
        reciprocal_matrix,
        lax.all_gather(partition_height.astype(jnp.bfloat16), "col", axis=0, tiled=True),
        preferred_element_type=jnp.float32,
    )
    return lax.psum(partial_value, "row")


def make_term(panel_tiles, white_bf):
    return jnp.einsum("tij,jk->itk", panel_tiles, white_bf, preferred_element_type=jnp.float32)


def body(
    member_outputs, pivot_inverse_matrices, former_subdiagonal_tiles, latter_subdiagonal_tiles
):
    starting_cheap_cholesky = standardize_prior_deviations(
        member_outputs[0], pivot_inverse_matrices[0]
    ).astype(jnp.bfloat16)
    coming = lax.psum_scatter(
        make_term(former_subdiagonal_tiles[:1], starting_cheap_cholesky),
        "col",
        scatter_dimension=0,
        tiled=True,
    )
    next_rows = member_outputs[1] - coming[:, 0]
    later_narrow_piece = standardize_prior_deviations(next_rows, pivot_inverse_matrices[1]).astype(
        jnp.bfloat16
    )
    remainder = lax.psum_scatter(
        make_term(former_subdiagonal_tiles[1:], starting_cheap_cholesky),
        "col",
        scatter_dimension=0,
        tiled=True,
    )
    later_rows = member_outputs[2:] - jnp.swapaxes(remainder, 0, 1)
    second_sum = lax.psum_scatter(
        make_term(latter_subdiagonal_tiles, later_narrow_piece),
        "col",
        scatter_dimension=0,
        tiled=True,
    )
    trailing = later_rows - jnp.swapaxes(second_sum, 0, 1)
    whitened = jnp.stack([starting_cheap_cholesky, later_narrow_piece])
    members = starting_cheap_cholesky.shape[1] // 2
    partial_value = jnp.einsum(
        "ie,ik->ek",
        starting_cheap_cholesky[:, :members],
        starting_cheap_cholesky,
        preferred_element_type=jnp.float32,
    )
    partial_value = partial_value + jnp.einsum(
        "ie,ik->ek",
        later_narrow_piece[:, :members],
        later_narrow_piece,
        preferred_element_type=jnp.float32,
    )
    projections = lax.psum(partial_value, "col")
    return (whitened, trailing, projections)


def solution(mesh):
    in_specs = (
        P(None, ("row", "col"), None),
        P(None, "col", "row"),
        P(None, "row", "col"),
        P(None, "row", "col"),
    )
    out_specs = (P(None, "col", None), P(None, ("row", "col"), None), P())
    return jax.shard_map(body, mesh=mesh, in_specs=in_specs, out_specs=out_specs, check_vma=False)
```

profile of v0, /device:TPU:16, one launch (start us, length us, event | category | flops | bytes accessed | tf_op | source)
XLA Modules:
  0.0 411.8 jit_solution(14639143338994882080)
XLA Ops:
  7.2 1.8 slice.67
  9.1 30.8 %all-gather.6.cloned.1.call-done = bf16[1,2048,512]{2,1,0:T(8,128)(2,1)} async-done(((bf16[1,256,512]{2,1,0:T(8,128)(2,1)}), bf16[1,2048,512]{2,1,0:T(8,128)(2,1)}) %all-gather.6.cloned.1.call-update) | async-done | bytes 2097168 | tf_op jit(solution)/shard_map/all_gather | solution.py:10
  39.9 5.2 %fusion.8 = f32[1024,512]{1,0:T(8,128)S(1)} fusion(bf16[2,1024,2048]{2,1,0:T(8,128)(2,1)} %param.5, bf16[1,2048,512]{2,1,0:T(8,128)(2,1)} %all-gather.6.cloned.1.call-done), kind=kOutput, calls=%fused_computation.8 | convolution fusion | flops 2147483648 | bytes 8388608 | tf_op jit(solution)/shard_map/dot_general | solution.py:8
  45.1 75.9 %all-reduce.5 = bf16[1024,512]{1,0:T(8,128)(2,1)S(1)} all-reduce(f32[1024,512]{1,0:T(8,128)S(1)} %fusion.8), channel_id=1, replica_groups=mesh['row'=4,'col'=8] {'row'}, use_global_device_ids=true, to_apply=%region_0.0 | all-reduce | flops 524288 | bytes 3145728 | tf_op jit(solution)/shard_map/psum | solution.py:13
  121.0 6.5 %fusion.14 = f32[2048,1,512]{0,2,1:T(8,128)} fusion(bf16[1024,512]{1,0:T(8,128)(2,1)S(1)} %all-reduce.5, bf16[2,2048,1024]{2,1,0:T(8,128)(2,1)} %param.6), kind=kOutput, calls=%fused_computation.14 | convolution fusion | flops 2147483648 | bytes 9437184 | tf_op jit(solution)/shard_map/tij,jk->itk/dot_general | solution.py:17
  127.5 0.0 all-gather.4.cloned.1.call-start
  127.6 1.3 fusion.31
  128.9 0.2 copy.12
  129.1 44.6 %reduce-scatter.4.cloned.1.call-done = f32[256,1,512]{0,2,1:T(8,128)} async-done(((f32[2048,1,512]{0,2,1:T(8,128)}), f32[256,1,512]{0,2,1:T(8,128)}) %reduce-scatter.4.cloned.1.call-update) | async-done | bytes 524304 | tf_op jit(solution)/shard_map/reduce_scatter | solution.py:26
  173.7 1.8 fusion.30
  175.6 6.5 %fusion.17 = f32[2048,1,512]{0,2,1:T(8,128)} fusion(bf16[1024,512]{1,0:T(8,128)(2,1)S(1)} %all-reduce.5, bf16[2,2048,1024]{2,1,0:T(8,128)(2,1)} %param.6), kind=kOutput, calls=%fused_computation.15 | convolution fusion | flops 2147483648 | bytes 9437184 | tf_op jit(solution)/shard_map/tij,jk->itk/dot_general | solution.py:17
  182.2 23.8 %all-gather.4.cloned.1.call-done = bf16[2048,512]{0,1:T(8,128)(2,1)} async-done(((bf16[256,512]{0,1:T(8,128)(2,1)}), bf16[2048,512]{0,1:T(8,128)(2,1)}) %all-gather.4.cloned.1.call-update) | async-done | bytes 2097168 | tf_op jit(solution)/shard_map/all_gather | solution.py:10
  206.0 6.5 %fusion.24 = f32[1024,512]{1,0:T(8,128)} fusion(bf16[2048,512]{0,1:T(8,128)(2,1)} %all-gather.4.cloned.1.call-done, bf16[2,1024,2048]{2,1,0:T(8,128)(2,1)} %param.5), kind=kOutput, calls=%fused_computation.19 | convolution fusion | flops 2147483648 | bytes 8388608 | tf_op jit(solution)/shard_map/dot_general | solution.py:8
  212.5 76.8 %all-reduce.6 = bf16[1024,512]{1,0:T(8,128)(2,1)S(1)} all-reduce(f32[1024,512]{1,0:T(8,128)} %fusion.24), channel_id=1, replica_groups=mesh['row'=4,'col'=8] {'row'}, use_global_device_ids=true, to_apply=%region_2.0 | all-reduce | flops 524288 | bytes 3145728 | tf_op jit(solution)/shard_map/psum | solution.py:13
  289.3 6.5 %fusion.20 = f32[2048,1,512]{0,2,1:T(8,128)} fusion(bf16[1024,512]{1,0:T(8,128)(2,1)S(1)} %all-reduce.6, bf16[1,2048,1024]{2,1,0:T(8,128)(2,1)} %param.7), kind=kOutput, calls=%fused_computation.16 | convolution fusion | flops 2147483648 | bytes 9437184 | tf_op jit(solution)/shard_map/tij,jk->itk/dot_general | solution.py:17
  295.9 0.2 copy.13
  296.1 0.5 fusion.28
  296.6 1.3 convolution_add_fusion
  297.8 1.5 pad_maximum_fusion
  299.4 44.8 %reduce-scatter.8.cloned.1.call-done = f32[256,1,512]{0,2,1:T(8,128)} async-done(((f32[2048,1,512]{0,2,1:T(8,128)}), f32[256,1,512]{0,2,1:T(8,128)}) %reduce-scatter.8.cloned.1.call-update) | async-done | bytes 524304 | tf_op jit(solution)/shard_map/reduce_scatter | solution.py:43
  344.2 1.3 bitcast_subtract_fusion
  345.5 1.0 copy.10
  346.5 56.6 %all-reduce.4.cloned.1.call-done = f32[256,512]{1,0:T(8,128)} async-done(((f32[256,512]{1,0:T(8,128)}), f32[256,512]{1,0:T(8,128)}) %all-reduce.4.cloned.1.call-update) | async-done | bytes 524304 | tf_op jit(solution)/shard_map/psum | solution.py:64
  403.1 1.9 copy.19
  (12 shorter events, 0.3 us)
Async XLA Ops:
  7.2 32.7 %all-gather.6.cloned.1.call-start = ((), (), s32[]{:S(2)}) async-start(), calls=%async_computation.8 | async-start | bytes 2359296 | tf_op jit(solution)/shard_map/all_gather | solution.py:10
  9.0 164.7 %reduce-scatter.4.cloned.1.call-start = ((), (), s32[]{:S(2)}) async-start(), calls=%async_computation.3 | async-start | bytes 4718592 | tf_op jit(solution)/shard_map/reduce_scatter | solution.py:26
  127.5 78.5 %all-gather.4.cloned.1.call-start = ((), (), s32[]{:S(2)}) async-start(), calls=%async_computation.4 | async-start | bytes 2359296 | tf_op jit(solution)/shard_map/all_gather | solution.py:10
  175.5 123.8 %reduce-scatter.6.cloned.1.call-start = ((), (), s32[]{:S(2)}) async-start(), calls=%async_computation.5 | async-start | bytes 4718592 | tf_op jit(solution)/shard_map/reduce_scatter | solution.py:36
  182.1 162.1 %reduce-scatter.8.cloned.1.call-start = ((), (), s32[]{:S(2)}) async-start(), calls=%async_computation.6 | async-start | bytes 4718592 | tf_op jit(solution)/shard_map/reduce_scatter | solution.py:43
  295.8 107.2 %all-reduce.4.cloned.1.call-start = ((), (), s32[]{:S(2)}) async-start(), calls=%async_computation.7 | async-start | bytes 1048576 | tf_op jit(solution)/shard_map/psum | solution.py:64
Sparse Core Ops, SparseCore 0:
  10.2 29.6 all-gather.5
  127.7 45.9 reduce-scatter.3
  175.9 30.0 all-gather.3
  208.1 48.1 reduce-scatter.5
  296.0 48.1 reduce-scatter.7
  346.9 56.0 all-reduce.3
where the time goes:
time: 415 us; the launch traced here: 412 us
  waiting for transfers between devices  201 us (48%)
  blocking collectives  153 us (37%)
  matrix products  33 us (8%)
  between operations  14.2 us (3%)
  local copies, waits for them, and re-layouts  6.31 us (2%)
  other arithmetic  4.6 us (1%)
    psum x2, blocking collectives, standardize_prior_deviations(): return lax.psum(partial_value, 'row')  153 us
    psum x1, waiting for transfers between devices, body(): projections = lax.psum(partial_value, 'col')  56.6 us
    all_gather x2, waiting for transfers between devices, standardize_prior_deviations(): lax.all_gather(partition_height.astype(jnp.bfloat16), 'col', axis=0, tile...  54.7 us
    reduce_scatter x1, waiting for transfers between devices, body(): lax.psum_scatter(make_term(latter_subdiagonal_tiles, later_narrow_piece),...  44.8 us
    reduce_scatter x1, waiting for transfers between devices, body(): lax.psum_scatter(make_term(former_subdiagonal_tiles[:1], starting_cheap_c...  44.6 us
    dot_general x3, matrix products, make_term(): jnp.einsum('tij,jk->itk', panel_tiles, white_bf, preferred_element_type=j...  19.6 us
    dot_general x2, matrix products, standardize_prior_deviations(): jnp.dot(reciprocal_matrix, lax.all_gather(partition_height.astype(jnp.bfl...  11.7 us
  transfers between devices with their start and end apart: 6, of which 5 were waited for; matrix products, arithmetic and copies ran while one was open for 6% of the time, Pallas kernels for 0%

commit v1 on v0

v1 whole, which is shorter than its diff:
```python
import functools

import jax
import jax.numpy as jnp
from jax import lax
from jax.experimental import pallas as pl
from jax.experimental.pallas import tpu as pltpu
from jax.sharding import PartitionSpec as P

MESH = pl.DeviceIdType.MESH
BF = jnp.bfloat16
F32 = jnp.float32
CHUNKS = 2


def kernel(
    R, Z, b, n, e,
    m_h, p_h, f_h, l_h,
    wh_out, tr_out, pr_out,
    m_v, p_v, f_v, l_v, xg, rs_s, rs_r, wv, acc, acc2, ps_s, ps_r, zs_s, zs_r, tr_v,
    pacc, pp_r, pz, pg,
    ld_sem, out_sem, po_sem,
    xz_s, xz_r, xp_s, xp_r, ra_s, ra_r, rb_s, rb_r, pa_s, pa_r, za_s, za_r,
    q_s, q_r, qz_s, qz_r, qr_s, qr_r,
):
    r = lax.axis_index("row")
    c = lax.axis_index("col")
    z = lax.div(c, 2)
    k = lax.rem(c, 2)
    rb, kb = R * b, 2 * Z * b
    partner = (r, z * 2 + 1 - k)

    def zpeer(zz):
        return (r, zz * 2 + k)

    def zz_of(d):
        return lax.rem(z + d, Z)

    def rr_of(d):
        return lax.rem(r + d, R)

    def rows(block, size, count=None):
        return pl.ds(pl.multiple_of(block * size, size), size if count is None else count)

    loads = {}

    def load(name, index, src, dst):
        copy = pltpu.make_async_copy(src, dst, ld_sem.at[index])
        copy.start()
        loads[name] = copy

    load("m", 0, m_h, m_v)
    load("p0", 1, p_h.at[0], p_v.at[0])
    load("f0", 2, f_h.at[0], f_v.at[0])
    load("p1", 3, p_h.at[1], p_v.at[1])
    load("f1", 4, f_h.at[1], f_v.at[1])
    load("l", 5, l_h.at[0], l_v.at[0])

    barrier = pltpu.get_barrier_semaphore()
    peers = [partner] + [zpeer(zz_of(d)) for d in range(1, Z)]
    peers += [(rr_of(d), c) for d in range(1, R)]
    for peer in peers:
        pl.semaphore_signal(barrier, inc=1, device_id=peer, device_id_type=MESH)
    pl.semaphore_wait(barrier, len(peers))

    sends = []
    local = []

    def send(src, dst, ssem, rsem, device):
        copy = pltpu.make_async_remote_copy(
            src_ref=src, dst_ref=dst, send_sem=ssem, recv_sem=rsem,
            device_id=device, device_id_type=MESH,
        )
        copy.start()
        sends.append(copy)

    def arrived(dst, ssem, rsem):
        pltpu.make_async_remote_copy(
            src_ref=dst, dst_ref=dst, send_sem=ssem, recv_sem=rsem,
            device_id=partner, device_id_type=MESH,
        ).wait_recv()

    waited = set()

    def ready(name):
        if name not in waited:
            waited.add(name)
            loads[name].wait()

    def matmul(a, x, total, put):
        tile = min(512, total)

        def step(i, carry):
            at = pl.ds(pl.multiple_of(i * tile, tile), tile)
            put(at, jnp.dot(a[at, :], x[...], preferred_element_type=F32))
            return carry

        lax.fori_loop(0, total // tile, step, 0)

    def xblock(s, j, cc):
        return xg.at[s, j, rows(cc, b), :]

    def give_x(s, j):
        mine = xblock(s, j, c)
        for d in range(1, Z):
            send(mine, mine, xz_s.at[s, j, d], xz_r.at[s, j, z], zpeer(zz_of(d)))
        send(mine, mine, xp_s.at[s, j, z], xp_r.at[s, j, z], partner)

    def p0(j):
        xg[0, j, rows(c, b), :] = m_v[0, :, j * n:(j + 1) * n].astype(BF)
        give_x(0, j)

    def p1(s, j):
        for d in range(1, Z):
            zz = zz_of(d)
            blk = xblock(s, j, zz * 2 + k)
            arrived(blk, xz_s.at[s, j, d], xz_r.at[s, j, zz])
            send(blk, blk, xp_s.at[s, j, zz], xp_r.at[s, j, zz], partner)

    def p2(s, j):
        for d in range(Z):
            zz = zz_of(d)
            arrived(xblock(s, j, zz * 2 + 1 - k), xp_s.at[s, j, zz], xp_r.at[s, j, zz])
        ready("p%d" % s)

        def put(at, value):
            acc[j, at, :] = value
            rs_s[s, j, at, :] = value.astype(BF)

        matmul(p_v.at[s], xg.at[s, j], rb, put)
        for d in range(1, R):
            rr = rr_of(d)
            send(rs_s.at[s, j, rows(rr, b), :], rs_r.at[s, j, r],
                 ra_s.at[s, j, d], ra_r.at[s, j, r], (rr, c))

    def p3(s, j):
        total = acc[j, rows(r, b), :]
        for d in range(1, R):
            rr = rr_of(d)
            arrived(rs_r.at[s, j, rr], ra_s.at[s, j, d], ra_r.at[s, j, rr])
            total = total + rs_r[s, j, rr].astype(F32)
        wv[s, j, rows(r, b), :] = total.astype(BF)
        mine = wv.at[s, j, rows(r, b), :]
        for d in range(1, R):
            send(mine, mine, rb_s.at[s, j, d], rb_r.at[s, j, r], (rr_of(d), c))

    def p4_wait(s, j):
        for d in range(1, R):
            rr = rr_of(d)
            arrived(wv.at[s, j, rows(rr, b), :], rb_s.at[s, j, d], rb_r.at[s, j, rr])
        copy = pltpu.make_async_copy(
            wv.at[s, j], wh_out.at[s, :, pl.ds(j * n, n)], out_sem.at[s, j])
        copy.start()
        local.append(copy)

    def p4(s, j):
        if s == 0:
            ready("f0")

            def put(at, value):
                acc[j, at, :] = value

            matmul(f_v.at[0], wv.at[s, j], kb, put)
        else:
            ready("l")

            def put(at, value):
                acc[j, at, :] = acc2[j, at, :] + value

            matmul(l_v.at[0], wv.at[s, j], kb, put)
        for zz in range(Z):
            ps_s[s, j, zz] = acc[j, rows(zz * 2 + 1 - k, b), :].astype(BF)
        send(ps_s.at[s, j], ps_r.at[s, j], pa_s.at[s, j], pa_r.at[s, j], partner)

    def p5(s, j):
        arrived(ps_r.at[s, j], pa_s.at[s, j], pa_r.at[s, j])
        for d in range(1, Z):
            zz = zz_of(d)
            value = acc[j, rows(zz * 2 + k, b), :] + ps_r[s, j, zz].astype(F32)
            zs_s[s, j, zz] = value.astype(BF)
            send(zs_s.at[s, j, zz], zs_r.at[s, j, z],
                 za_s.at[s, j, d], za_r.at[s, j, z], zpeer(zz))
        if s == 0:
            ready("f1")

            def put(at, value):
                acc2[j, at, :] = value

            matmul(f_v.at[1], wv.at[0, j], kb, put)

    def p6(s, j):
        total = acc[j, rows(c, b), :] + ps_r[s, j, z].astype(F32)
        for d in range(1, Z):
            zz = zz_of(d)
            arrived(zs_r.at[s, j, zz], za_s.at[s, j, d], za_r.at[s, j, zz])
            total = total + zs_r[s, j, zz].astype(F32)
        value = m_v[s + 1, :, j * n:(j + 1) * n] - total
        if s == 0:
            xg[1, j, rows(c, b), :] = value.astype(BF)
            give_x(1, j)
        else:
            tr_v[:, j * n:(j + 1) * n] = value

    h = e // R // 2

    def gram(s):
        for j in range(CHUNKS):
            value = lax.dot_general(
                wv[s, 0], wv[s, j], (((0,), (0,)), ((), ())), preferred_element_type=F32)
            at = slice(j * n, (j + 1) * n)
            if s == 0:
                pacc[:, at] = value
            else:
                pacc[:, at] = pacc[:, at] + value

    def q0():
        gram(1)
        send(pacc.at[rows(r * 2 + 1 - k, h), :], pp_r, q_s.at[0], q_r.at[0], partner)

    def q1():
        arrived(pp_r, q_s.at[0], q_r.at[0])
        pz[z] = pacc[rows(r * 2 + k, h), :] + pp_r[...]
        for d in range(1, Z):
            send(pz.at[z], pz.at[z], qz_s.at[d], qz_r.at[z], zpeer(zz_of(d)))

    def q2():
        for d in range(1, Z):
            zz = zz_of(d)
            arrived(pz.at[zz], qz_s.at[d], qz_r.at[zz])
        total = pz[0]
        for zz in range(1, Z):
            total = total + pz[zz]
        pg[k, r] = total
        mine = pg.at[k, r]
        for d in range(1, R):
            send(mine, mine, qr_s.at[d], qr_r.at[r], (rr_of(d), c))

    def q3():
        for d in range(1, R):
            rr = rr_of(d)
            arrived(pg.at[k, rr], qr_s.at[d], qr_r.at[rr])
        send(pg.at[k], pg.at[k], q_s.at[1], q_r.at[1], partner)

    def q4():
        arrived(pg.at[1 - k], q_s.at[1], q_r.at[1])
        for kk in range(2):
            copy = pltpu.make_async_copy(pg.at[kk], pr_out.at[:, kk], po_sem.at[kk])
            copy.start()
            local.append(copy)

    def full4(s, j):
        p4_wait(s, j)
        p4(s, j)

    A, B = 0, 1
    ready("m")
    p0(A)
    p0(B)
    p1(0, A)
    p2(0, A)
    p3(0, A)
    p1(0, B)
    p2(0, B)
    full4(0, A)
    p5(0, A)
    p3(0, B)
    full4(0, B)
    p6(0, A)
    p5(0, B)
    gram(0)
    p1(1, A)
    p2(1, A)
    p3(1, A)
    p6(0, B)
    full4(1, A)
    p5(1, A)
    p1(1, B)
    p2(1, B)
    p3(1, B)
    p6(1, A)
    p4_wait(1, B)
    q0()
    p4(1, B)
    q1()
    p5(1, B)
    q2()
    q3()
    p6(1, B)
    copy = pltpu.make_async_copy(tr_v, tr_out.at[0], po_sem.at[2])
    copy.start()
    local.append(copy)
    q4()
    for copy in sends:
        copy.wait_send()
    for copy in local:
        copy.wait()


def body(R, Z, m, p, f, l):
    b, cols = m.shape[1], m.shape[2]
    n = cols // CHUNKS
    e = cols // 2
    rb, kb = R * b, 2 * Z * b
    h = e // R // 2
    sem = pltpu.SemaphoreType.DMA
    V = pltpu.VMEM
    flops = 2 * 5 * rb * kb * cols
    any_spec = pl.BlockSpec(memory_space=pl.ANY)
    whitened, trailing, proj = pl.pallas_call(
        functools.partial(kernel, R, Z, b, n, e),
        out_shape=(
            jax.ShapeDtypeStruct((2, rb, cols), BF),
            jax.ShapeDtypeStruct((1, b, cols), F32),
            jax.ShapeDtypeStruct((R, 2, h, cols), F32),
        ),
        in_specs=[any_spec] * 4,
        out_specs=(any_spec,) * 3,
        scratch_shapes=[
            V(m.shape, F32), V(p.shape, BF), V(f.shape, BF), V(l.shape, BF),
            V((2, CHUNKS, kb, n), BF),
            V((2, CHUNKS, rb, n), BF), V((2, CHUNKS, R, b, n), BF),
            V((2, CHUNKS, rb, n), BF),
            V((CHUNKS, kb, n), F32), V((CHUNKS, kb, n), F32),
            V((2, CHUNKS, Z, b, n), BF), V((2, CHUNKS, Z, b, n), BF),
            V((2, CHUNKS, Z, b, n), BF), V((2, CHUNKS, Z, b, n), BF),
            V((b, cols), F32),
            V((e, cols), F32), V((h, cols), F32), V((Z, h, cols), F32),
            V((2, R, h, cols), F32),
            sem((6,)), sem((2, CHUNKS)), sem((3,)),
            sem((2, CHUNKS, Z)), sem((2, CHUNKS, Z)),
            sem((2, CHUNKS, Z)), sem((2, CHUNKS, Z)),
            sem((2, CHUNKS, R)), sem((2, CHUNKS, R)),
            sem((2, CHUNKS, R)), sem((2, CHUNKS, R)),
            sem((2, CHUNKS)), sem((2, CHUNKS)),
            sem((2, CHUNKS, Z)), sem((2, CHUNKS, Z)),
            sem((2,)), sem((2,)), sem((Z,)), sem((Z,)), sem((R,)), sem((R,)),
        ],
        compiler_params=pltpu.CompilerParams(
            collective_id=0, has_side_effects=True, vmem_limit_bytes=60 * 2**20),
        cost_estimate=pl.CostEstimate(
            flops=flops, bytes_accessed=10 * rb * kb, transcendentals=0),
    )(m, p, f, l)
    return whitened, trailing, proj.reshape(e, cols)


def solution(mesh):
    R, Z = mesh.shape["row"], mesh.shape["col"] // 2
    in_specs = (
        P(None, ("row", "col"), None),
        P(None, "col", "row"),
        P(None, "row", "col"),
        P(None, "row", "col"),
    )
    out_specs = (P(None, "col", None), P(None, ("row", "col"), None), P())
    return jax.shard_map(
        functools.partial(body, R, Z), mesh=mesh, in_specs=in_specs, out_specs=out_specs,
        check_vma=False,
    )
```

time: 415 us -> 143 us (0.34)
  waiting for transfers between devices: 201 us -> 0 us
  blocking collectives: 153 us -> 0 us
  Pallas kernels: 0 us -> 136 us
  matrix products: 33 us -> 0 us
  between operations: 14.2 us -> 0.66 us
  other arithmetic: 4.6 us -> 0 us
    psum x2 -> x0, blocking collectives: 153 us -> none  [standardize_prior_deviations(): return lax.psum(partial_value, 'row')]
    pallas_call x0 -> x1, Pallas kernels: none -> 136 us  [body(): pl.pallas_call(functools.partial(kernel, R, Z, b, n, e), out_shape=(jax.S...]
    reduce_scatter x3 -> x0, waiting for transfers between devices: 89.4 us -> none  [the longest x1 44.8 us: body(): lax.psum_scatter(make_term(latter_subdiagonal_tiles, later_narrow_piece),...]
    psum x1 -> x0, waiting for transfers between devices: 56.6 us -> none  [body(): projections = lax.psum(partial_value, 'col')]
    all_gather x2 -> x0, waiting for transfers between devices: 54.7 us -> none  [standardize_prior_deviations(): lax.all_gather(partition_height.astype(jnp.bfloat16), 'col', axis=0, tile...]
    dot_general x7 -> x0, matrix products: 33 us -> none  [the longest x3 19.6 us: make_term(): jnp.einsum('tij,jk->itk', panel_tiles, white_bf, preferred_element_type=j...]
  transfers between devices with their start and end apart: 6 -> 0, of which waited for: 5 -> 0; matrix products, arithmetic and copies ran while one was open for 6% -> 0% of each run, Pallas kernels for 0% -> 0%
where the time goes in v1:
time: 143 us; the launch traced here: 142 us
  Pallas kernels  136 us (95%)
  local copies, waits for them, and re-layouts  4.73 us (3%)
    pallas_call x1, Pallas kernels, body(): pl.pallas_call(functools.partial(kernel, R, Z, b, n, e), out_shape=(jax.S...  136 us
    unnamed x7, local copies, waits for them, and re-layouts  4.73 us

profile of v1, /device:TPU:16, one launch (start us, length us, event | category | flops | bytes accessed | tf_op | source)
XLA Modules:
  0.0 141.8 jit_solution(11574012426715010171)
XLA Ops:
  0.6 136.5 %shard_map.67 = (bf16[2,1024,512]{2,1,0:T(8,128)(2,1)}, f32[1,256,512]{2,1,0:T(8,128)}, f32[4,2,32,512]{3,2,1,0:T(8,128)}) custom-call(f32[3,256,512]{2,1,0:T(8,128)} %m_h.1, bf16[2,1024,2048]{2,1,0:T(8,128)(2,1)} %p_h.1, bf16[2,2048,1024]{2,1,0:T(8,128)(2,1)} %f_h.1, bf16[1,2048,1024]{2,1,0:T(8,128)(2,1)} %l_h.1), custom_call_target="tpu_custom_call" | custom-call | flops 10737418240 | bytes 20971520 | tf_op jit(solution)/shard_map/pallas_call | solution.py:309
  137.1 0.0 copy-start.1
  137.1 0.0 copy-start
  137.1 3.1 %copy.10 = bf16[2,1024,512]{2,1,0:T(8,128)(2,1)} copy(bf16[2,1024,512]{2,1,0:T(8,128)(2,1)} %get-tuple-element.12) | data formatting | bytes 4194304
  140.2 0.0 copy-done.1
  140.2 0.8 copy.11
  141.0 0.0 copy-done
  141.0 0.8 copy.12
Async XLA Ops:
  137.1 3.2 %copy-start.1 = (f32[1,256,512]{2,1,0:T(8,128)S(1)}, f32[1,256,512]{2,1,0:T(8,128)}, u32[]{:S(2)}) copy-start(f32[1,256,512]{2,1,0:T(8,128)} %get-tuple-element.13) | copy-start | bytes 1572868
  137.1 3.9 %copy-start = (f32[4,2,32,512]{3,2,1,0:T(8,128)S(1)}, f32[4,2,32,512]{3,2,1,0:T(8,128)}, u32[]{:S(2)}) copy-start(f32[4,2,32,512]{3,2,1,0:T(8,128)} %get-tuple-element.8) | copy-start | bytes 1572868

commit v2 on v1

--- a/solution.py
+++ b/solution.py
@@ -18,10 +18,10 @@
     m_h, p_h, f_h, l_h,
     wh_out, tr_out, pr_out,
     m_v, p_v, f_v, l_v, xg, rs_s, rs_r, wv, acc, acc2, ps_s, ps_r, zs_s, zs_r, tr_v,
-    pacc, pp_r, pz, pg,
+    pacc, pp_r, pz, pg, zi_r,
     ld_sem, out_sem, po_sem,
     xz_s, xz_r, xp_s, xp_r, ra_s, ra_r, rb_s, rb_r, pa_s, pa_r, za_s, za_r,
-    q_s, q_r, qz_s, qz_r, qr_s, qr_r,
+    q_s, q_r, qz_s, qz_r, qr_s, qr_r, io_s, io_r, t_s, t_r,
 ):
     r = lax.axis_index("row")
     c = lax.axis_index("col")
@@ -33,6 +33,13 @@
     def zpeer(zz):
         return (r, zz * 2 + k)
 
+    left = z < Z // 2
+    edge = (z == 0) | (z == Z - 1)
+    mid = (z == Z // 2 - 1) | (z == Z // 2)
+    mid_slot = jnp.where(mid, 1, 0)
+    inward = zpeer(jnp.where(left, z + 1, z - 1))
+    outward = zpeer(jnp.where(left, jnp.maximum(z - 1, 0), jnp.minimum(z + 1, Z - 1)))
+
     def zz_of(d):
         return lax.rem(z + d, Z)
 
@@ -66,13 +73,14 @@
     sends = []
     local = []
 
-    def send(src, dst, ssem, rsem, device):
+    def send(src, dst, ssem, rsem, device, into=None):
         copy = pltpu.make_async_remote_copy(
             src_ref=src, dst_ref=dst, send_sem=ssem, recv_sem=rsem,
             device_id=device, device_id_type=MESH,
         )
         copy.start()
-        sends.append(copy)
+        if into is None:
+            sends.append(copy)
 
     def arrived(dst, ssem, rsem):
         pltpu.make_async_remote_copy(
@@ -172,34 +180,66 @@
             ps_s[s, j, zz] = acc[j, rows(zz * 2 + 1 - k, b), :].astype(BF)
         send(ps_s.at[s, j], ps_r.at[s, j], pa_s.at[s, j], pa_r.at[s, j], partner)
 
-    def p5(s, j):
+    def f1(j):
+        ready("f1")
+
+        def put(at, value):
+            acc2[j, at, :] = value
+
+        matmul(f_v.at[1], wv.at[0, j], kb, put)
+
+    def pair(s, j):
         arrived(ps_r.at[s, j], pa_s.at[s, j], pa_r.at[s, j])
+
+    def s1(j, q):
+        at = rows(q * 2 + k, b)
+        own = jnp.where(z == q, m_v[1, :, j * n:(j + 1) * n], 0.0)
+        acc[j, at, :] = acc[j, at, :] + ps_r[0, j, q].astype(F32) - own
+
+        @pl.when(jnp.logical_not(edge))
+        def _():
+            arrived(zi_r.at[0, j, q], io_s.at[j, q], io_r.at[0, j, q])
+            acc[j, at, :] = acc[j, at, :] + zi_r[0, j, q].astype(F32)
+
+        zs_s[0, j, q] = acc[j, at, :].astype(BF)
+        send(zs_s.at[0, j, q], zi_r.at[mid_slot, j, q],
+             io_s.at[j, q], io_r.at[mid_slot, j, q], inward)
+
+    def s2(j, q):
+        at = rows(q * 2 + k, b)
+        blk = xg.at[1, j, at, :]
+
+        @pl.when(mid)
+        def _():
+            arrived(zi_r.at[1, j, q], io_s.at[j, q], io_r.at[1, j, q])
+            xg[1, j, at, :] = (-(acc[j, at, :] + zi_r[1, j, q].astype(F32))).astype(BF)
+
+        @pl.when(jnp.logical_not(mid))
+        def _():
+            arrived(blk, t_s.at[j, q], t_r.at[j, q])
+
+        @pl.when(jnp.logical_not(edge))
+        def _():
+            send(blk, blk, t_s.at[j, q], t_r.at[j, q], outward, False)
+
+        send(blk, blk, xp_s.at[1, j, q], xp_r.at[1, j, q], partner)
+
+    def p5(j):
+        pair(1, j)
         for d in range(1, Z):
             zz = zz_of(d)
-            value = acc[j, rows(zz * 2 + k, b), :] + ps_r[s, j, zz].astype(F32)
-            zs_s[s, j, zz] = value.astype(BF)
-            send(zs_s.at[s, j, zz], zs_r.at[s, j, z],
-                 za_s.at[s, j, d], za_r.at[s, j, z], zpeer(zz))
-        if s == 0:
-            ready("f1")
-
-            def put(at, value):
-                acc2[j, at, :] = value
-
-            matmul(f_v.at[1], wv.at[0, j], kb, put)
-
-    def p6(s, j):
-        total = acc[j, rows(c, b), :] + ps_r[s, j, z].astype(F32)
+            value = acc[j, rows(zz * 2 + k, b), :] + ps_r[1, j, zz].astype(F32)
+            zs_s[1, j, zz] = value.astype(BF)
+            send(zs_s.at[1, j, zz], zs_r.at[j, z],
+                 za_s.at[j, d], za_r.at[j, z], zpeer(zz))
+
+    def p6(j):
+        total = acc[j, rows(c, b), :] + ps_r[1, j, z].astype(F32)
         for d in range(1, Z):
             zz = zz_of(d)
-            arrived(zs_r.at[s, j, zz], za_s.at[s, j, d], za_r.at[s, j, zz])
-            total = total + zs_r[s, j, zz].astype(F32)
-        value = m_v[s + 1, :, j * n:(j + 1) * n] - total
-        if s == 0:
-            xg[1, j, rows(c, b), :] = value.astype(BF)
-            give_x(1, j)
-        else:
-            tr_v[:, j * n:(j + 1) * n] = value
+            arrived(zs_r.at[j, zz], za_s.at[j, d], za_r.at[j, zz])
+            total = total + zs_r[j, zz].astype(F32)
+        tr_v[:, j * n:(j + 1) * n] = m_v[2, :, j * n:(j + 1) * n] - total
 
     h = e // R // 2
 
@@ -254,44 +294,69 @@
 
     A, B = 0, 1
     ready("m")
+    half = (Z + 1) // 2
     p0(A)
+    p1(0, A)
     p0(B)
-    p1(0, A)
     p2(0, A)
     p3(0, A)
     p1(0, B)
     p2(0, B)
     full4(0, A)
-    p5(0, A)
+    pair(0, A)
+    s1(A, 0)
+    f1(A)
     p3(0, B)
+    for q in range(1, Z - 1):
+        s1(A, q)
     full4(0, B)
-    p6(0, A)
-    p5(0, B)
+    s1(A, Z - 1)
+    for q in range(half):
+        s2(A, q)
+    pair(0, B)
+    s1(B, 0)
+    for q in range(half, Z):
+        s2(A, q)
+    s1(B, 1)
+    p2(1, A)
+    for q in range(2, Z):
+        s1(B, q)
+    s2(B, 0)
+    p3(1, A)
+    for q in range(1, Z):
+        s2(B, q)
+    f1(B)
+    full4(1, A)
+    p2(1, B)
+    p5(A)
     gram(0)
-    p1(1, A)
-    p2(1, A)
-    p3(1, A)
-    p6(0, B)
-    full4(1, A)
-    p5(1, A)
-    p1(1, B)
-    p2(1, B)
     p3(1, B)
-    p6(1, A)
     p4_wait(1, B)
     q0()
     p4(1, B)
     q1()
-    p5(1, B)
+    p6(A)
+    p5(B)
     q2()
     q3()
-    p6(1, B)
+    p6(B)
     copy = pltpu.make_async_copy(tr_v, tr_out.at[0], po_sem.at[2])
     copy.start()
     local.append(copy)
     q4()
     for copy in sends:
         copy.wait_send()
+
+    @pl.when(jnp.logical_not(edge))
+    def _():
+        for j in range(CHUNKS):
+            for q in range(Z):
+                blk = xg.at[1, j, rows(q * 2 + k, b), :]
+                pltpu.make_async_remote_copy(
+                    src_ref=blk, dst_ref=blk, send_sem=t_s.at[j, q], recv_sem=t_r.at[j, q],
+                    device_id=outward, device_id_type=MESH,
+                ).wait_send()
+
     for copy in local:
         copy.wait()
 
@@ -322,18 +387,19 @@
             V((2, CHUNKS, rb, n), BF),
             V((CHUNKS, kb, n), F32), V((CHUNKS, kb, n), F32),
             V((2, CHUNKS, Z, b, n), BF), V((2, CHUNKS, Z, b, n), BF),
-            V((2, CHUNKS, Z, b, n), BF), V((2, CHUNKS, Z, b, n), BF),
+            V((2, CHUNKS, Z, b, n), BF), V((CHUNKS, Z, b, n), BF),
             V((b, cols), F32),
             V((e, cols), F32), V((h, cols), F32), V((Z, h, cols), F32),
-            V((2, R, h, cols), F32),
+            V((2, R, h, cols), F32), V((2, CHUNKS, Z, b, n), BF),
             sem((6,)), sem((2, CHUNKS)), sem((3,)),
             sem((2, CHUNKS, Z)), sem((2, CHUNKS, Z)),
             sem((2, CHUNKS, Z)), sem((2, CHUNKS, Z)),
             sem((2, CHUNKS, R)), sem((2, CHUNKS, R)),
             sem((2, CHUNKS, R)), sem((2, CHUNKS, R)),
             sem((2, CHUNKS)), sem((2, CHUNKS)),
-            sem((2, CHUNKS, Z)), sem((2, CHUNKS, Z)),
+            sem((CHUNKS, Z)), sem((CHUNKS, Z)),
             sem((2,)), sem((2,)), sem((Z,)), sem((Z,)), sem((R,)), sem((R,)),
+            sem((CHUNKS, Z)), sem((2, CHUNKS, Z)), sem((CHUNKS, Z)), sem((CHUNKS, Z)),
         ],
         compiler_params=pltpu.CompilerParams(
             collective_id=0, has_side_effects=True, vmem_limit_bytes=60 * 2**20),

time: 143 us -> 140 us (0.979)
    pallas_call x1, Pallas kernels: 136 us -> 135 us  [body(): pl.pallas_call(functools.partial(kernel, R, Z, b, n, e), out_shape=(jax.S...]
where the time goes in v2:
time: 140 us
  Pallas kernels  135 us (96%)
  local copies, waits for them, and re-layouts  4.73 us (3%)
    pallas_call x1, Pallas kernels, body(): pl.pallas_call(functools.partial(kernel, R, Z, b, n, e), out_shape=(jax.S...  135 us
    unnamed x7, local copies, waits for them, and re-layouts  4.73 us

profile of v2, /device:TPU:16, one launch (start us, length us, event | category | flops | bytes accessed | tf_op | source)
XLA Modules:
  0.0 140.2 jit_solution(13207080344638259993)
XLA Ops:
  0.6 134.8 %shard_map.67 = (bf16[2,1024,512]{2,1,0:T(8,128)(2,1)}, f32[1,256,512]{2,1,0:T(8,128)}, f32[4,2,32,512]{3,2,1,0:T(8,128)}) custom-call(f32[3,256,512]{2,1,0:T(8,128)} %m_h.1, bf16[2,1024,2048]{2,1,0:T(8,128)(2,1)} %p_h.1, bf16[2,2048,1024]{2,1,0:T(8,128)(2,1)} %f_h.1, bf16[1,2048,1024]{2,1,0:T(8,128)(2,1)} %l_h.1), custom_call_target="tpu_custom_call" | custom-call | flops 10737418240 | bytes 20971520 | tf_op jit(solution)/shard_map/pallas_call | solution.py:374
  135.4 0.0 copy-start.1
  135.4 0.0 copy-start
  135.4 3.1 %copy.10 = bf16[2,1024,512]{2,1,0:T(8,128)(2,1)} copy(bf16[2,1024,512]{2,1,0:T(8,128)(2,1)} %get-tuple-element.12) | data formatting | bytes 4194304
  138.6 0.0 copy-done.1
  138.6 0.8 copy.11
  139.4 0.0 copy-done
  139.4 0.8 copy.12
Async XLA Ops:
  135.4 3.2 %copy-start.1 = (f32[1,256,512]{2,1,0:T(8,128)S(1)}, f32[1,256,512]{2,1,0:T(8,128)}, u32[]{:S(2)}) copy-start(f32[1,256,512]{2,1,0:T(8,128)} %get-tuple-element.13) | copy-start | bytes 1572868
  135.4 3.9 %copy-start = (f32[4,2,32,512]{3,2,1,0:T(8,128)S(1)}, f32[4,2,32,512]{3,2,1,0:T(8,128)}, u32[]{:S(2)}) copy-start(f32[4,2,32,512]{3,2,1,0:T(8,128)} %get-tuple-element.8) | copy-start | bytes 1572868

commit v3 on v2

--- a/solution.py
+++ b/solution.py
@@ -18,7 +18,7 @@
     m_h, p_h, f_h, l_h,
     wh_out, tr_out, pr_out,
     m_v, p_v, f_v, l_v, xg, rs_s, rs_r, wv, acc, acc2, ps_s, ps_r, zs_s, zs_r, tr_v,
-    pacc, pp_r, pz, pg, zi_r,
+    pacc, pp_r, pz, pg, zi_r, accp,
     ld_sem, out_sem, po_sem,
     xz_s, xz_r, xp_s, xp_r, ra_s, ra_r, rb_s, rb_r, pa_s, pa_r, za_s, za_r,
     q_s, q_r, qz_s, qz_r, qr_s, qr_r, io_s, io_r, t_s, t_r,
@@ -118,31 +118,56 @@
         xg[0, j, rows(c, b), :] = m_v[0, :, j * n:(j + 1) * n].astype(BF)
         give_x(0, j)
 
-    def p1(s, j):
-        for d in range(1, Z):
-            zz = zz_of(d)
-            blk = xblock(s, j, zz * 2 + k)
-            arrived(blk, xz_s.at[s, j, d], xz_r.at[s, j, zz])
-            send(blk, blk, xp_s.at[s, j, zz], xp_r.at[s, j, zz], partner)
-
-    def p2(s, j):
-        for d in range(Z):
-            zz = zz_of(d)
-            arrived(xblock(s, j, zz * 2 + 1 - k), xp_s.at[s, j, zz], xp_r.at[s, j, zz])
+    def from_z(s, j, d):
+        zz = zz_of(d)
+        blk = xblock(s, j, zz * 2 + k)
+        arrived(blk, xz_s.at[s, j, d], xz_r.at[s, j, zz])
+        send(blk, blk, xp_s.at[s, j, zz], xp_r.at[s, j, zz], partner)
+
+    split = (2 * b) % 128 == 0
+
+    def columns(zz):
+        return pl.ds(pl.multiple_of(zz * 2 * b, 2 * b), 2 * b) if split else slice(None)
+
+    def taken(s, j, zz):
+        return xg.at[s, j, rows(zz, 2 * b), :] if split else xg.at[s, j]
+
+    def kblock(s, j, zz, first):
+        arrived(xblock(s, j, zz * 2 + 1 - k), xp_s.at[s, j, zz], xp_r.at[s, j, zz])
         ready("p%d" % s)
-
-        def put(at, value):
-            acc[j, at, :] = value
-            rs_s[s, j, at, :] = value.astype(BF)
-
-        matmul(p_v.at[s], xg.at[s, j], rb, put)
-        for d in range(1, R):
+        if split:
+            def put(at, value):
+                accp[j, at, :] = value if first else accp[j, at, :] + value
+
+            matmul(p_v.at[s, :, columns(zz)], taken(s, j, zz), rb, put)
+
+    def klast(s, j, zz):
+        arrived(xblock(s, j, zz * 2 + 1 - k), xp_s.at[s, j, zz], xp_r.at[s, j, zz])
+        ready("p%d" % s)
+        for d in list(range(1, R)) + [0]:
             rr = rr_of(d)
-            send(rs_s.at[s, j, rows(rr, b), :], rs_r.at[s, j, r],
-                 ra_s.at[s, j, d], ra_r.at[s, j, r], (rr, c))
+            at = rows(rr, b)
+            value = jnp.dot(p_v[s, at, columns(zz)], taken(s, j, zz)[...],
+                            preferred_element_type=F32)
+            if split and Z > 1:
+                value = accp[j, at, :] + value
+            if d:
+                rs_s[s, j, at, :] = value.astype(BF)
+                send(rs_s.at[s, j, at, :], rs_r.at[s, j, r],
+                     ra_s.at[s, j, d], ra_r.at[s, j, r], (rr, c))
+            else:
+                accp[j, at, :] = value
+
+    def gather(j):
+        for d in range(1, Z):
+            from_z(0, j, d)
+            kblock(0, j, zz_of(d - 1), d == 1)
+
+    def first_product(j):
+        klast(0, j, zz_of(Z - 1))
 
     def p3(s, j):
-        total = acc[j, rows(r, b), :]
+        total = accp[j, rows(r, b), :]
         for d in range(1, R):
             rr = rr_of(d)
             arrived(rs_r.at[s, j, rr], ra_s.at[s, j, d], ra_r.at[s, j, rr])
@@ -161,24 +186,23 @@
         copy.start()
         local.append(copy)
 
+    def tile(s, j, block):
+        at = rows(block, b)
+        if s == 0:
+            return jnp.dot(f_v[0, at, :], wv[0, j], preferred_element_type=F32)
+        return acc2[j, at, :] + jnp.dot(l_v[0, at, :], wv[1, j], preferred_element_type=F32)
+
     def p4(s, j):
-        if s == 0:
-            ready("f0")
-
-            def put(at, value):
-                acc[j, at, :] = value
-
-            matmul(f_v.at[0], wv.at[s, j], kb, put)
-        else:
-            ready("l")
-
-            def put(at, value):
-                acc[j, at, :] = acc2[j, at, :] + value
-
-            matmul(l_v.at[0], wv.at[s, j], kb, put)
-        for zz in range(Z):
-            ps_s[s, j, zz] = acc[j, rows(zz * 2 + 1 - k, b), :].astype(BF)
-        send(ps_s.at[s, j], ps_r.at[s, j], pa_s.at[s, j], pa_r.at[s, j], partner)
+        ready("l" if s else "f0")
+        for i in range(Z):
+            q = zz_of(1 + i) if s else i
+            ps_s[s, j, q] = tile(s, j, q * 2 + 1 - k).astype(BF)
+            send(ps_s.at[s, j, q], ps_r.at[s, j, q], pa_s.at[s, j, q], pa_r.at[s, j, q], partner)
+
+    def paired(s, j, q):
+        value = tile(s, j, q * 2 + k)
+        arrived(ps_r.at[s, j, q], pa_s.at[s, j, q], pa_r.at[s, j, q])
+        return value + ps_r[s, j, q].astype(F32)
 
     def f1(j):
         ready("f1")
@@ -187,14 +211,11 @@
             acc2[j, at, :] = value
 
         matmul(f_v.at[1], wv.at[0, j], kb, put)
-
-    def pair(s, j):
-        arrived(ps_r.at[s, j], pa_s.at[s, j], pa_r.at[s, j])
 
     def s1(j, q):
         at = rows(q * 2 + k, b)
         own = jnp.where(z == q, m_v[1, :, j * n:(j + 1) * n], 0.0)
-        acc[j, at, :] = acc[j, at, :] + ps_r[0, j, q].astype(F32) - own
+        acc[j, at, :] = paired(0, j, q) - own
 
         @pl.when(jnp.logical_not(edge))
         def _():
@@ -225,16 +246,15 @@
         send(blk, blk, xp_s.at[1, j, q], xp_r.at[1, j, q], partner)
 
     def p5(j):
-        pair(1, j)
         for d in range(1, Z):
             zz = zz_of(d)
-            value = acc[j, rows(zz * 2 + k, b), :] + ps_r[1, j, zz].astype(F32)
-            zs_s[1, j, zz] = value.astype(BF)
+            zs_s[1, j, zz] = paired(1, j, zz).astype(BF)
             send(zs_s.at[1, j, zz], zs_r.at[j, z],
                  za_s.at[j, d], za_r.at[j, z], zpeer(zz))
+        acc[j, rows(c, b), :] = paired(1, j, z)
 
     def p6(j):
-        total = acc[j, rows(c, b), :] + ps_r[1, j, z].astype(F32)
+        total = acc[j, rows(c, b), :]
         for d in range(1, Z):
             zz = zz_of(d)
             arrived(zs_r.at[j, zz], za_s.at[j, d], za_r.at[j, zz])
@@ -295,48 +315,53 @@
     A, B = 0, 1
     ready("m")
     half = (Z + 1) // 2
+
+    def back(j, q):
+        s2(j, q)
+        if q:
+            kblock(1, j, q - 1, q == 1)
+
     p0(A)
-    p1(0, A)
+    gather(A)
     p0(B)
-    p2(0, A)
+    first_product(A)
     p3(0, A)
-    p1(0, B)
-    p2(0, B)
+    gather(B)
+    first_product(B)
     full4(0, A)
-    pair(0, A)
     s1(A, 0)
-    f1(A)
     p3(0, B)
     for q in range(1, Z - 1):
         s1(A, q)
     full4(0, B)
     s1(A, Z - 1)
     for q in range(half):
-        s2(A, q)
-    pair(0, B)
+        back(A, q)
     s1(B, 0)
     for q in range(half, Z):
-        s2(A, q)
+        back(A, q)
     s1(B, 1)
-    p2(1, A)
+    klast(1, A, Z - 1)
     for q in range(2, Z):
         s1(B, q)
-    s2(B, 0)
+    f1(A)
+    back(B, 0)
     p3(1, A)
     for q in range(1, Z):
-        s2(B, q)
+        back(B, q)
+    p4_wait(1, A)
+    p4(1, A)
+    klast(1, B, Z - 1)
+    p5(A)
     f1(B)
-    full4(1, A)
-    p2(1, B)
-    p5(A)
+    p3(1, B)
     gram(0)
-    p3(1, B)
     p4_wait(1, B)
+    p4(1, B)
     q0()
-    p4(1, B)
+    p5(B)
     q1()
     p6(A)
-    p5(B)
     q2()
     q3()
     p6(B)
@@ -358,6 +383,18 @@
                 ).wait_send()
 
     for copy in local:
+        copy.wait()
+
+
+def hand_over(*refs):
+    count = len(refs) // 2
+    sems = refs[-1]
+    copies = [
+        pltpu.make_async_copy(refs[i], refs[count + i], sems.at[i]) for i in range(count)
+    ]
+    for copy in copies:
+        copy.start()
+    for copy in copies:
         copy.wait()
 
 
@@ -390,13 +427,13 @@
             V((2, CHUNKS, Z, b, n), BF), V((CHUNKS, Z, b, n), BF),
             V((b, cols), F32),
             V((e, cols), F32), V((h, cols), F32), V((Z, h, cols), F32),
-            V((2, R, h, cols), F32), V((2, CHUNKS, Z, b, n), BF),
+            V((2, R, h, cols), F32), V((2, CHUNKS, Z, b, n), BF), V((CHUNKS, rb, n), F32),
             sem((6,)), sem((2, CHUNKS)), sem((3,)),
             sem((2, CHUNKS, Z)), sem((2, CHUNKS, Z)),
             sem((2, CHUNKS, Z)), sem((2, CHUNKS, Z)),
             sem((2, CHUNKS, R)), sem((2, CHUNKS, R)),
             sem((2, CHUNKS, R)), sem((2, CHUNKS, R)),
-            sem((2, CHUNKS)), sem((2, CHUNKS)),
+            sem((2, CHUNKS, Z)), sem((2, CHUNKS, Z)),
             sem((CHUNKS, Z)), sem((CHUNKS, Z)),
             sem((2,)), sem((2,)), sem((Z,)), sem((Z,)), sem((R,)), sem((R,)),
             sem((CHUNKS, Z)), sem((2, CHUNKS, Z)), sem((CHUNKS, Z)), sem((CHUNKS, Z)),
@@ -406,7 +443,14 @@
         cost_estimate=pl.CostEstimate(
             flops=flops, bytes_accessed=10 * rb * kb, transcendentals=0),
     )(m, p, f, l)
-    return whitened, trailing, proj.reshape(e, cols)
+    results = (whitened, trailing, proj.reshape(e, cols))
+    return pl.pallas_call(
+        hand_over,
+        out_shape=tuple(jax.ShapeDtypeStruct(a.shape, a.dtype) for a in results),
+        in_specs=[any_spec] * 3,
+        out_specs=(any_spec,) * 3,
+        scratch_shapes=[sem((3,))],
+    )(*results)
 
 
 def solution(mesh):

time: 140 us -> 244 us (1.74); the launches traced: 140 us -> 241 us
  Pallas kernels: 135 us -> 241 us
  local copies, waits for them, and re-layouts: 4.73 us -> 0 us
    pallas_call x0 -> x1, Pallas kernels: none -> 96.4 us  [body(): pl.pallas_call(hand_over, out_shape=tuple((jax.ShapeDtypeStruct(a.shape,...]
    pallas_call x1, Pallas kernels: 135 us -> 144 us  [body(): pl.pallas_call(functools.partial(kernel, R, Z, b, n, e), out_shape=(jax.S...]
    unnamed x7 -> x0, local copies, waits for them, and re-layouts: 4.73 us -> none
where the time goes in v3:
time: 244 us; the launch traced here: 241 us
  Pallas kernels  241 us (99%)
    pallas_call x1, Pallas kernels, body(): pl.pallas_call(functools.partial(kernel, R, Z, b, n, e), out_shape=(jax.S...  144 us
    pallas_call x1, Pallas kernels, body(): pl.pallas_call(hand_over, out_shape=tuple((jax.ShapeDtypeStruct(a.shape,...  96.4 us

profile of v3, /device:TPU:16, one launch (start us, length us, event | category | flops | bytes accessed | tf_op | source)
XLA Modules:
  0.0 241.4 jit_solution(9445468405094961857)
XLA Ops:
  0.6 144.1 %shard_map.67 = (bf16[2,1024,512]{2,1,0:T(8,128)(2,1)}, f32[1,256,512]{2,1,0:T(8,128)}, f32[4,2,32,512]{3,2,1,0:T(8,128)}) custom-call(f32[3,256,512]{2,1,0:T(8,128)} %m_h.1, bf16[2,1024,2048]{2,1,0:T(8,128)(2,1)} %p_h.1, bf16[2,2048,1024]{2,1,0:T(8,128)(2,1)} %f_h.1, bf16[1,2048,1024]{2,1,0:T(8,128)(2,1)} %l_h.1), custom_call_target="tpu_custom_call" | custom-call | flops 10737418240 | bytes 20971520 | tf_op jit(solution)/shard_map/pallas_call | solution.py:411
  144.8 96.4 %shard_map.68 = (bf16[2,1024,512]{2,1,0:T(8,128)(2,1)}, f32[1,256,512]{2,1,0:T(8,128)}, f32[256,512]{1,0:T(8,128)}) custom-call(bf16[2,1024,512]{2,1,0:T(8,128)(2,1)} %get-tuple-element.6.refs_0_, f32[1,256,512]{2,1,0:T(8,128)} %get-tuple-element.7.refs_1_, f32[256,512]{1,0:T(8,128)} %bitcast.1), custom_call_target="tpu_custom_call" | custom-call | tf_op jit(solution)/shard_map/pallas_call | solution.py:447

commit v4 on v2

--- a/solution.py
+++ b/solution.py
@@ -95,15 +95,40 @@
             waited.add(name)
             loads[name].wait()
 
-    def matmul(a, x, total, put):
+    def matmul(a, x, dst, total, depth, init=True):
         tile = min(512, total)
+        block = min(256, depth)
+
+        def one(i, carry):
+            at = pl.ds(pl.multiple_of(i * tile, tile), tile)
+
+            def first(q, carry):
+                dst[pl.ds(pl.multiple_of(i * tile + q * 16, 16), 16), :] = jnp.zeros((16, n), F32)
+                return carry
+
+            if init:
+                lax.fori_loop(0, tile // 16, first, 0)
+
+            def step(q, carry):
+                deep = pl.ds(pl.multiple_of(q * block, block), block)
+                dst[at, :] += jnp.dot(a[at, deep], x[deep, :], preferred_element_type=F32)
+                return carry
+
+            return lax.fori_loop(0, depth // block, step, carry)
+
+        lax.fori_loop(0, total // tile, one, 0)
+
+    def pieces(count, fn):
+        size = min(32, b)
 
         def step(i, carry):
-            at = pl.ds(pl.multiple_of(i * tile, tile), tile)
-            put(at, jnp.dot(a[at, :], x[...], preferred_element_type=F32))
+            def at(start=0):
+                return pl.ds(pl.multiple_of(start + i * size, 16), size)
+
+            fn(at)
             return carry
 
-        lax.fori_loop(0, total // tile, step, 0)
+        lax.fori_loop(0, count // size, step, 0)
 
     def xblock(s, j, cc):
         return xg.at[s, j, rows(cc, b), :]
@@ -115,7 +140,10 @@
         send(mine, mine, xp_s.at[s, j, z], xp_r.at[s, j, z], partner)
 
     def p0(j):
-        xg[0, j, rows(c, b), :] = m_v[0, :, j * n:(j + 1) * n].astype(BF)
+        def fn(at):
+            xg[0, j, at(c * b), :] = m_v[0, at(), j * n:(j + 1) * n].astype(BF)
+
+        pieces(b, fn)
         give_x(0, j)
 
     def p1(s, j):
@@ -131,23 +159,29 @@
             arrived(xblock(s, j, zz * 2 + 1 - k), xp_s.at[s, j, zz], xp_r.at[s, j, zz])
         ready("p%d" % s)
 
-        def put(at, value):
-            acc[j, at, :] = value
-            rs_s[s, j, at, :] = value.astype(BF)
-
-        matmul(p_v.at[s], xg.at[s, j], rb, put)
+        matmul(p_v.at[s], xg.at[s, j], acc.at[j], rb, kb)
+
+        def fn(at):
+            rs_s[s, j, at(), :] = acc[j, at(), :].astype(BF)
+
+        pieces(rb, fn)
         for d in range(1, R):
             rr = rr_of(d)
             send(rs_s.at[s, j, rows(rr, b), :], rs_r.at[s, j, r],
                  ra_s.at[s, j, d], ra_r.at[s, j, r], (rr, c))
 
     def p3(s, j):
-        total = acc[j, rows(r, b), :]
         for d in range(1, R):
             rr = rr_of(d)
             arrived(rs_r.at[s, j, rr], ra_s.at[s, j, d], ra_r.at[s, j, rr])
-            total = total + rs_r[s, j, rr].astype(F32)
-        wv[s, j, rows(r, b), :] = total.astype(BF)
+
+        def fn(at):
+            total = acc[j, at(r * b), :]
+            for d in range(1, R):
+                total = total + rs_r[s, j, rr_of(d), at(), :].astype(F32)
+            wv[s, j, at(r * b), :] = total.astype(BF)
+
+        pieces(b, fn)
         mine = wv.at[s, j, rows(r, b), :]
         for d in range(1, R):
             send(mine, mine, rb_s.at[s, j, d], rb_r.at[s, j, r], (rr_of(d), c))
@@ -162,46 +196,48 @@
         local.append(copy)
 
     def p4(s, j):
+        ready("l" if s else "f0")
         if s == 0:
-            ready("f0")
-
-            def put(at, value):
-                acc[j, at, :] = value
-
-            matmul(f_v.at[0], wv.at[s, j], kb, put)
+            matmul(f_v.at[0], wv.at[s, j], acc.at[j], kb, rb)
         else:
-            ready("l")
-
-            def put(at, value):
-                acc[j, at, :] = acc2[j, at, :] + value
-
-            matmul(l_v.at[0], wv.at[s, j], kb, put)
-        for zz in range(Z):
-            ps_s[s, j, zz] = acc[j, rows(zz * 2 + 1 - k, b), :].astype(BF)
+            matmul(l_v.at[0], wv.at[s, j], acc2.at[j], kb, rb, init=False)
+        full = acc2 if s else acc
+
+        def fn(at):
+            for zz in range(Z):
+                ps_s[s, j, zz, at(), :] = full[j, at((zz * 2 + 1 - k) * b), :].astype(BF)
+
+        pieces(b, fn)
         send(ps_s.at[s, j], ps_r.at[s, j], pa_s.at[s, j], pa_r.at[s, j], partner)
 
     def f1(j):
         ready("f1")
 
-        def put(at, value):
-            acc2[j, at, :] = value
-
-        matmul(f_v.at[1], wv.at[0, j], kb, put)
+        matmul(f_v.at[1], wv.at[0, j], acc2.at[j], kb, rb)
 
     def pair(s, j):
         arrived(ps_r.at[s, j], pa_s.at[s, j], pa_r.at[s, j])
 
     def s1(j, q):
-        at = rows(q * 2 + k, b)
-        own = jnp.where(z == q, m_v[1, :, j * n:(j + 1) * n], 0.0)
-        acc[j, at, :] = acc[j, at, :] + ps_r[0, j, q].astype(F32) - own
+        at0 = (q * 2 + k) * b
+        keep = jnp.where(z == q, 1.0, 0.0)
 
         @pl.when(jnp.logical_not(edge))
         def _():
             arrived(zi_r.at[0, j, q], io_s.at[j, q], io_r.at[0, j, q])
-            acc[j, at, :] = acc[j, at, :] + zi_r[0, j, q].astype(F32)
-
-        zs_s[0, j, q] = acc[j, at, :].astype(BF)
+
+            def fn(at):
+                acc[j, at(at0), :] += zi_r[0, j, q, at(), :].astype(F32)
+
+            pieces(b, fn)
+
+        def fn(at):
+            value = acc[j, at(at0), :] + ps_r[0, j, q, at(), :].astype(F32)
+            value = value - keep * m_v[1, at(), j * n:(j + 1) * n]
+            acc[j, at(at0), :] = value
+            zs_s[0, j, q, at(), :] = value.astype(BF)
+
+        pieces(b, fn)
         send(zs_s.at[0, j, q], zi_r.at[mid_slot, j, q],
              io_s.at[j, q], io_r.at[mid_slot, j, q], inward)
 
@@ -212,7 +248,13 @@
         @pl.when(mid)
         def _():
             arrived(zi_r.at[1, j, q], io_s.at[j, q], io_r.at[1, j, q])
-            xg[1, j, at, :] = (-(acc[j, at, :] + zi_r[1, j, q].astype(F32))).astype(BF)
+
+            def fn(piece):
+                at0 = (q * 2 + k) * b
+                total = acc[j, piece(at0), :] + zi_r[1, j, q, piece(), :].astype(F32)
+                xg[1, j, piece(at0), :] = (-total).astype(BF)
+
+            pieces(b, fn)
 
         @pl.when(jnp.logical_not(mid))
         def _():
@@ -228,30 +270,46 @@
         pair(1, j)
         for d in range(1, Z):
             zz = zz_of(d)
-            value = acc[j, rows(zz * 2 + k, b), :] + ps_r[1, j, zz].astype(F32)
-            zs_s[1, j, zz] = value.astype(BF)
+
+            def fn(at):
+                value = acc2[j, at((zz * 2 + k) * b), :] + ps_r[1, j, zz, at(), :].astype(F32)
+                zs_s[1, j, zz, at(), :] = value.astype(BF)
+
+            pieces(b, fn)
             send(zs_s.at[1, j, zz], zs_r.at[j, z],
                  za_s.at[j, d], za_r.at[j, z], zpeer(zz))
 
     def p6(j):
-        total = acc[j, rows(c, b), :] + ps_r[1, j, z].astype(F32)
         for d in range(1, Z):
             zz = zz_of(d)
             arrived(zs_r.at[j, zz], za_s.at[j, d], za_r.at[j, zz])
-            total = total + zs_r[j, zz].astype(F32)
-        tr_v[:, j * n:(j + 1) * n] = m_v[2, :, j * n:(j + 1) * n] - total
+
+        def fn(at):
+            total = acc2[j, at(c * b), :] + ps_r[1, j, z, at(), :].astype(F32)
+            for d in range(1, Z):
+                total = total + zs_r[j, zz_of(d), at(), :].astype(F32)
+            cols = slice(j * n, (j + 1) * n)
+            tr_v[at(), cols] = m_v[2, at(), cols] - total
+
+        pieces(b, fn)
 
     h = e // R // 2
 
     def gram(s):
         for j in range(CHUNKS):
-            value = lax.dot_general(
-                wv[s, 0], wv[s, j], (((0,), (0,)), ((), ())), preferred_element_type=F32)
-            at = slice(j * n, (j + 1) * n)
+            cols = slice(j * n, (j + 1) * n)
+            block = min(256, rb)
             if s == 0:
-                pacc[:, at] = value
-            else:
-                pacc[:, at] = pacc[:, at] + value
+                pacc[:, cols] = jnp.zeros((e, n), F32)
+
+            def step(q, carry):
+                at = pl.ds(pl.multiple_of(q * block, block), block)
+                pacc[:, cols] += lax.dot_general(
+                    wv[s, 0, at, :], wv[s, j, at, :], (((0,), (0,)), ((), ())),
+                    preferred_element_type=F32)
+                return carry
+
+            lax.fori_loop(0, rb // block, step, 0)
 
     def q0():
         gram(1)
@@ -361,6 +419,18 @@
         copy.wait()
 
 
+def hand_over(*refs):
+    count = len(refs) // 2
+    sems = refs[-1]
+    copies = [
+        pltpu.make_async_copy(refs[i], refs[count + i], sems.at[i]) for i in range(count)
+    ]
+    for copy in copies:
+        copy.start()
+    for copy in copies:
+        copy.wait()
+
+
 def body(R, Z, m, p, f, l):
     b, cols = m.shape[1], m.shape[2]
     n = cols // CHUNKS
@@ -406,7 +476,14 @@
         cost_estimate=pl.CostEstimate(
             flops=flops, bytes_accessed=10 * rb * kb, transcendentals=0),
     )(m, p, f, l)
-    return whitened, trailing, proj.reshape(e, cols)
+    results = (whitened, trailing, proj.reshape(e, cols))
+    return pl.pallas_call(
+        hand_over,
+        out_shape=tuple(jax.ShapeDtypeStruct(a.shape, a.dtype) for a in results),
+        in_specs=[any_spec] * 3,
+        out_specs=(any_spec,) * 3,
+        scratch_shapes=[sem((3,))],
+    )(*results)
 
 
 def solution(mesh):

time: 140 us -> 257 us (1.84)
  Pallas kernels: 135 us -> 257 us
  local copies, waits for them, and re-layouts: 4.73 us -> 0 us
    pallas_call x0 -> x1, Pallas kernels: none -> 96.4 us  [body(): pl.pallas_call(hand_over, out_shape=tuple((jax.ShapeDtypeStruct(a.shape,...]
    pallas_call x1, Pallas kernels: 135 us -> 160 us  [body(): pl.pallas_call(functools.partial(kernel, R, Z, b, n, e), out_shape=(jax.S...]
    unnamed x7 -> x0, local copies, waits for them, and re-layouts: 4.73 us -> none
where the time goes in v4:
time: 257 us
  Pallas kernels  257 us (100%)
    pallas_call x1, Pallas kernels, body(): pl.pallas_call(functools.partial(kernel, R, Z, b, n, e), out_shape=(jax.S...  160 us
    pallas_call x1, Pallas kernels, body(): pl.pallas_call(hand_over, out_shape=tuple((jax.ShapeDtypeStruct(a.shape,...  96.4 us

profile of v4, /device:TPU:16, one launch (start us, length us, event | category | flops | bytes accessed | tf_op | source)
XLA Modules:
  0.0 257.1 jit_solution(16068643061943742677)
XLA Ops:
  0.6 160.1 %shard_map.67 = (bf16[2,1024,512]{2,1,0:T(8,128)(2,1)}, f32[1,256,512]{2,1,0:T(8,128)}, f32[4,2,32,512]{3,2,1,0:T(8,128)}) custom-call(f32[3,256,512]{2,1,0:T(8,128)} %m_h.1, bf16[2,1024,2048]{2,1,0:T(8,128)(2,1)} %p_h.1, bf16[2,2048,1024]{2,1,0:T(8,128)(2,1)} %f_h.1, bf16[1,2048,1024]{2,1,0:T(8,128)(2,1)} %l_h.1), custom_call_target="tpu_custom_call" | custom-call | flops 10737418240 | bytes 20971520 | tf_op jit(solution)/shard_map/pallas_call | solution.py:444
  160.7 96.4 %shard_map.68 = (bf16[2,1024,512]{2,1,0:T(8,128)(2,1)}, f32[1,256,512]{2,1,0:T(8,128)}, f32[256,512]{1,0:T(8,128)}) custom-call(bf16[2,1024,512]{2,1,0:T(8,128)(2,1)} %get-tuple-element.6.refs_0_, f32[1,256,512]{2,1,0:T(8,128)} %get-tuple-element.7.refs_1_, f32[256,512]{1,0:T(8,128)} %bitcast.1), custom_call_target="tpu_custom_call" | custom-call | tf_op jit(solution)/shard_map/pallas_call | solution.py:480

commit v5 on v2

--- a/solution.py
+++ b/solution.py
@@ -96,7 +96,7 @@
             loads[name].wait()
 
     def matmul(a, x, total, put):
-        tile = min(512, total)
+        tile = min(1024, total)
 
         def step(i, carry):
             at = pl.ds(pl.multiple_of(i * tile, tile), tile)

time: 140 us -> 139 us (level)
  no operation moved by 1% of the time
where the time goes in v5:
time: 139 us
  Pallas kernels  134 us (96%)
  local copies, waits for them, and re-layouts  4.73 us (3%)
    pallas_call x1, Pallas kernels, body(): pl.pallas_call(functools.partial(kernel, R, Z, b, n, e), out_shape=(jax.S...  134 us
    unnamed x7, local copies, waits for them, and re-layouts  4.73 us

profile of v5, /device:TPU:16, one launch (start us, length us, event | category | flops | bytes accessed | tf_op | source)
XLA Modules:
  0.0 138.9 jit_solution(13815743144326807733)
XLA Ops:
  0.6 133.6 %shard_map.67 = (bf16[2,1024,512]{2,1,0:T(8,128)(2,1)}, f32[1,256,512]{2,1,0:T(8,128)}, f32[4,2,32,512]{3,2,1,0:T(8,128)}) custom-call(f32[3,256,512]{2,1,0:T(8,128)} %m_h.1, bf16[2,1024,2048]{2,1,0:T(8,128)(2,1)} %p_h.1, bf16[2,2048,1024]{2,1,0:T(8,128)(2,1)} %f_h.1, bf16[1,2048,1024]{2,1,0:T(8,128)(2,1)} %l_h.1), custom_call_target="tpu_custom_call" | custom-call | flops 10737418240 | bytes 20971520 | tf_op jit(solution)/shard_map/pallas_call | solution.py:374
  134.2 0.0 copy-start.1
  134.2 0.0 copy-start
  134.2 3.1 %copy.10 = bf16[2,1024,512]{2,1,0:T(8,128)(2,1)} copy(bf16[2,1024,512]{2,1,0:T(8,128)(2,1)} %get-tuple-element.12) | data formatting | bytes 4194304
  137.3 0.0 copy-done.1
  137.3 0.8 copy.11
  138.1 0.0 copy-done
  138.1 0.8 copy.12
Async XLA Ops:
  134.2 3.2 %copy-start.1 = (f32[1,256,512]{2,1,0:T(8,128)S(1)}, f32[1,256,512]{2,1,0:T(8,128)}, u32[]{:S(2)}) copy-start(f32[1,256,512]{2,1,0:T(8,128)} %get-tuple-element.13) | copy-start | bytes 1572868
  134.2 3.9 %copy-start = (f32[4,2,32,512]{3,2,1,0:T(8,128)S(1)}, f32[4,2,32,512]{3,2,1,0:T(8,128)}, u32[]{:S(2)}) copy-start(f32[4,2,32,512]{3,2,1,0:T(8,128)} %get-tuple-element.8) | copy-start | bytes 1572868
